TPU v7x, 256 devices: a whole 4x4x8 slice. The times are simulated.
256 devices in a mesh: row: 16 (over z, y_lo), col: 16 (over y_hi, x, core).
Axes of the slice: x: 4, y: 4 (y_hi: 2, y_lo: 2; y = y_hi * 2 + y_lo), z: 8, core: 2. Of those that a mesh axis runs over, the one named last changes fastest.
Arguments:
- paths_in: float32 [32768, 256], P(('row', 'col')), may hold values from 0.05 to 4
- dep_in: float32 [32768, 256], P(('row', 'col')), may hold values from 0 to 4
- levels: int32 [32768, 256], P(('row', 'col')), may hold values from 0 to 4, as said below
- tile_src: int32 [16, 16, 16, 4], P('row', 'col'), may hold values from 0 to 15, as said below
- pattern: int32 [16, 16, 16, 4, 128, 128], P('row', 'col'), may hold values from 0 to 1, as said below
Outputs:
- dependency: float32 [32768, 256], P(('row', 'col'))
Inputs may be any that keep to these rules, and one draw needn't show every extreme that they name: The value 4 marks a vertex outside the window's levels for that source. A program may send only the non-zero entries of a level's rounded path counts or backward weights, together with their positions, in any encoding that loses nothing. `tile_src`: within one device the 4 source tiles of a destination tile row are distinct, and every source tile index appears in exactly 4 of the device's slots. `pattern`: each slot holds either an all-zero tile or a tile of independent 0/1 entries; a device has from 1 to 64 nonzero tiles, and some device has all its slots nonzero.
All inputs are finite; a program needn't handle non-finite values.
Results may differ from a plain program's by a relative error of at most 0.0016.
Values may be sent and summed in bfloat16 or wider, within the bound.
A program may use at most 64 MiB of HBM per device.

v0:
```python
import jax
import jax.numpy as jnp
from jax import lax
from jax.sharding import PartitionSpec as P


def laid_out(blocks, dim):
    dims = list(blocks.shape[1:])
    dims[dim] *= blocks.shape[0]
    return jnp.moveaxis(blocks, 0, dim).reshape(dims)


def from_everyone(value, axis):
    copies = jnp.broadcast_to(value, (lax.axis_size(axis), *value.shape))
    return lax.all_to_all(copies, axis, split_axis=0, concat_axis=0, tiled=True)


def gather_directly(value, axis, dim):
    return laid_out(from_everyone(value, axis), dim)


def cut_along(value, dim, devices):
    dims = value.shape
    blocks = value.reshape(*dims[:dim], devices, dims[dim] // devices, *dims[dim + 1 :])
    return jnp.moveaxis(blocks, dim, 0)


def sent_and_summed(value, axis, dim):
    devices = lax.axis_size(axis)
    blocks = lax.all_to_all(cut_along(value, dim, devices), axis, 0, 0, tiled=True)
    return jnp.sum(blocks, axis=0)


def shards(paths_in, dep_in, levels, tile_src, pattern):
    vert_dev = paths_in.shape[0]
    tile_size = pattern.shape[-1]
    dest_tiles = tile_src.shape[2]
    band_slots = tile_src.shape[3]
    src_tiles = lax.axis_size("col") * vert_dev // tile_size
    per_source = dest_tiles * band_slots // src_tiles
    source_ids = tile_src[0, 0]
    tile_values = pattern[0, 0].astype(jnp.bfloat16)
    flat_ids = source_ids.reshape(-1)
    by_source = jnp.argsort(flat_ids, stable=True)
    back_values = tile_values.reshape(-1, tile_size, tile_size)[by_source]
    back_values = back_values.reshape(src_tiles, per_source, tile_size, tile_size)
    back_dest = (by_source // band_slots).reshape(src_tiles, per_source)

    def forward_terms(frontier):
        gathered = gather_directly(frontier, "col", 0)
        pieces = gathered.reshape(src_tiles, tile_size, gathered.shape[1])

        def dest_terms(begin_row, row_count):
            picked = pieces[source_ids]
            product = jnp.einsum(
                "ibrj,ibjs->irs", tile_values, picked, preferred_element_type=jnp.float32
            )
            return product.reshape(row_count, product.shape[2])

        return dest_terms

    def scattered(dest_terms):
        return sent_and_summed(dest_terms(jnp.int32(0), vert_dev * lax.axis_size("row")), "row", 0)

    def spread(weight):
        return gather_directly(weight, "row", 0)

    level_masks = [(levels == distance).astype(jnp.float32) for distance in range(4)]
    numerator = level_masks[3] * (1.0 + dep_in)
    path_counts = [level_masks[0] * paths_in]
    for distance in (1, 2):
        dest_terms = forward_terms(path_counts[-1].astype(jnp.bfloat16))
        path_counts.append(level_masks[distance] * scattered(dest_terms))
    last_terms = forward_terms(path_counts[-1].astype(jnp.bfloat16))
    paths_last = level_masks[3] * scattered(last_terms)
    spread_weight = spread((numerator / jnp.maximum(paths_last, 1.0)).astype(jnp.bfloat16))
    dependency = jnp.zeros(paths_in.shape, jnp.float32)
    for distance in (2, 1, 0):
        backward_pieces = spread_weight.reshape(dest_tiles, tile_size, spread_weight.shape[1])
        source_picked = backward_pieces[back_dest]
        source_product = jnp.einsum(
            "tgrj,tgrs->tjs", back_values, source_picked, preferred_element_type=jnp.float32
        )
        dependence = (
            level_masks[distance]
            * path_counts[distance]
            * sent_and_summed(
                source_product.reshape(vert_dev * lax.axis_size("col"), source_product.shape[2]),
                "col",
                0,
            )
        )
        dependency = dependency + dependence
        if distance > 0:
            weight = (
                level_masks[distance] * (1.0 + dependence) / jnp.maximum(path_counts[distance], 1.0)
            ).astype(jnp.bfloat16)
            spread_weight = spread(weight)
    return dependency


def solution(mesh):
    placed = (
        P(("row", "col"), None),
        P(("row", "col"), None),
        P(("row", "col"), None),
        P("row", "col", None, None),
        P("row", "col", None, None, None, None),
    )
    return jax.shard_map(
        shards, mesh=mesh, in_specs=placed, out_specs=P(("row", "col"), None), check_vma=False
    )
```

profile of v0, /device:TPU:1, one launch (start us, length us, event | category | flops | bytes accessed | tf_op | source)
XLA Modules:
  0.0 487.3 jit_solution(7561831118256897654)
XLA Ops:
  3.9 8.4 %all-to-all-start = ((bf16[16,128,256]{2,1,0:T(8,128)(2,1)}), bf16[16,128,256]{2,1,0:T(8,128)(2,1)S(1)}, u32[]{:S(2)}, u32[]{:S(2)}) async-start(bf16[16,128,256]{2,1,0:T(8,128)(2,1)} %broadcast_in_dim.27), calls=%async_computation | async-start | bytes 2097152 | tf_op jit(solution)/shard_map/all_to_all | solution.py:15
  15.2 14.5 %all-to-all-done = bf16[16,128,256]{2,1,0:T(8,128)(2,1)S(1)} async-done(((bf16[16,128,256]{2,1,0:T(8,128)(2,1)}), bf16[16,128,256]{2,1,0:T(8,128)(2,1)S(1)}, u32[]{:S(2)}, u32[]{:S(2)}) %all-to-all-start) | async-done | bytes 1048608 | tf_op jit(solution)/shard_map/all_to_all | solution.py:15
  29.7 2.7 gather_fusion
  32.4 3.5 fusion.6
  35.9 57.6 %all_to_all.60 = f32[16,128,256]{1,2,0:T(8,128)} all-to-all(f32[16,128,256]{1,2,0:T(8,128)S(1)} %fusion.6), channel_id=1, replica_groups=mesh['row'=16,'col'=16] {'row'}, dimensions={0} | all-to-all | bytes 4194304 | tf_op jit(solution)/shard_map/all_to_all | solution.py:30
  96.1 23.3 %all_to_all.61 = bf16[16,128,256]{2,1,0:T(8,128)(2,1)S(1)} all-to-all(bf16[16,128,256]{2,1,0:T(8,128)(2,1)S(1)} %broadcast_in_dim.28), channel_id=1, replica_groups=mesh['row'=16,'col'=16] {'col'}, dimensions={0} | all-to-all | bytes 2097152 | tf_op jit(solution)/shard_map/all_to_all | solution.py:15
  119.4 2.7 gather_fusion.1
  122.1 3.5 fusion.9
  125.6 52.6 %all_to_all.62 = f32[16,128,256]{1,2,0:T(8,128)} all-to-all(f32[16,128,256]{1,2,0:T(8,128)S(1)} %fusion.9), channel_id=1, replica_groups=mesh['row'=16,'col'=16] {'row'}, dimensions={0} | all-to-all | bytes 4194304 | tf_op jit(solution)/shard_map/all_to_all | solution.py:30
  180.8 23.2 %all_to_all.63 = bf16[16,128,256]{2,1,0:T(8,128)(2,1)S(1)} all-to-all(bf16[16,128,256]{2,1,0:T(8,128)(2,1)S(1)} %broadcast_in_dim.30), channel_id=1, replica_groups=mesh['row'=16,'col'=16] {'col'}, dimensions={0} | all-to-all | bytes 2097152 | tf_op jit(solution)/shard_map/all_to_all | solution.py:15
  204.0 2.7 gather_fusion.3
  206.7 4.9 fusion.12
  211.6 4.6 all-to-all-start.5
  216.3 47.9 %all-to-all-done.5 = f32[16,128,256]{1,2,0:T(8,128)} async-done(((f32[16,128,256]{1,2,0:T(8,128)}), f32[16,128,256]{1,2,0:T(8,128)}, u32[]{:S(2)}, u32[]{:S(2)}) %all-to-all-start.5) | async-done | bytes 2097184 | tf_op jit(solution)/shard_map/all_to_all | solution.py:30
  267.1 6.1 %all-to-all-start.6 = ((bf16[16,128,256]{2,1,0:T(8,128)(2,1)}), bf16[16,128,256]{2,1,0:T(8,128)(2,1)S(1)}, u32[]{:S(2)}, u32[]{:S(2)}) async-start(bf16[16,128,256]{2,1,0:T(8,128)(2,1)} %broadcast_in_dim.31), calls=%async_computation.6 | async-start | bytes 2097152 | tf_op jit(solution)/shard_map/all_to_all | solution.py:15
  278.1 20.4 %all-to-all-done.6 = bf16[16,128,256]{2,1,0:T(8,128)(2,1)S(1)} async-done(((bf16[16,128,256]{2,1,0:T(8,128)(2,1)}), bf16[16,128,256]{2,1,0:T(8,128)(2,1)S(1)}, u32[]{:S(2)}, u32[]{:S(2)}) %all-to-all-start.6) | async-done | bytes 1048608 | tf_op jit(solution)/shard_map/all_to_all | solution.py:15
  301.2 3.1 convolution_bitcast_fusion.2
  304.2 37.5 %all_to_all.64 = f32[16,128,256]{2,1,0:T(8,128)} all-to-all(f32[16,128,256]{2,1,0:T(8,128)S(1)} %convolution_bitcast_fusion.2), channel_id=1, replica_groups=mesh['row'=16,'col'=16] {'col'}, dimensions={0} | all-to-all | bytes 4194304 | tf_op jit(solution)/shard_map/all_to_all | solution.py:30
  343.8 29.5 %all_to_all.65 = bf16[16,128,256]{2,1,0:T(8,128)(2,1)S(1)} all-to-all(bf16[16,128,256]{2,1,0:T(8,128)(2,1)S(1)} %broadcast_in_dim.32), channel_id=1, replica_groups=mesh['row'=16,'col'=16] {'row'}, dimensions={0} | all-to-all | bytes 2097152 | tf_op jit(solution)/shard_map/all_to_all | solution.py:15
  376.0 3.1 convolution_bitcast_fusion.1
  379.1 34.7 %all_to_all.66 = f32[16,128,256]{2,1,0:T(8,128)} all-to-all(f32[16,128,256]{2,1,0:T(8,128)S(1)} %convolution_bitcast_fusion.1), channel_id=1, replica_groups=mesh['row'=16,'col'=16] {'col'}, dimensions={0} | all-to-all | bytes 4194304 | tf_op jit(solution)/shard_map/all_to_all | solution.py:30
  416.3 29.4 %all_to_all.67 = bf16[16,128,256]{2,1,0:T(8,128)(2,1)S(1)} all-to-all(bf16[16,128,256]{2,1,0:T(8,128)(2,1)S(1)} %broadcast_in_dim.33), channel_id=1, replica_groups=mesh['row'=16,'col'=16] {'row'}, dimensions={0} | all-to-all | bytes 2097152 | tf_op jit(solution)/shard_map/all_to_all | solution.py:15
  448.5 3.1 convolution_bitcast_fusion
  451.6 34.6 %all_to_all.68 = f32[16,128,256]{2,1,0:T(8,128)S(1)} all-to-all(f32[16,128,256]{2,1,0:T(8,128)S(1)} %convolution_bitcast_fusion), channel_id=1, replica_groups=mesh['row'=16,'col'=16] {'col'}, dimensions={0} | all-to-all | bytes 4194304 | tf_op jit(solution)/shard_map/all_to_all | solution.py:30
  (77 shorter events, 33.5 us)
Async XLA Ops:
  0.0 12.3 %copy-start.11 = (s32[1,1,16,4]{2,3,1,0:T(4,128)S(1)}, s32[1,1,16,4]{2,3,1,0:T(4,128)}, u32[]{:S(2)}) copy-start(s32[1,1,16,4]{2,3,1,0:T(4,128)} %param.8) | copy-start | bytes 772
  2.0 1.9 copy-start.1
  3.9 25.8 %all-to-all-start = ((bf16[16,128,256]{2,1,0:T(8,128)(2,1)}), bf16[16,128,256]{2,1,0:T(8,128)(2,1)S(1)}, u32[]{:S(2)}, u32[]{:S(2)}) async-start(bf16[16,128,256]{2,1,0:T(8,128)(2,1)} %broadcast_in_dim.27), calls=%async_computation | async-start | bytes 2097152 | tf_op jit(solution)/shard_map/all_to_all | solution.py:15
  211.6 4.6 copy-start.9
  211.6 52.6 %all-to-all-start.5 = ((f32[16,128,256]{1,2,0:T(8,128)}), f32[16,128,256]{1,2,0:T(8,128)}, u32[]{:S(2)}, u32[]{:S(2)}) async-start(f32[16,128,256]{1,2,0:T(8,128)} %fusion.12), calls=%async_computation.5 | async-start | bytes 4194304 | tf_op jit(solution)/shard_map/all_to_all | solution.py:30
  267.1 31.3 %all-to-all-start.6 = ((bf16[16,128,256]{2,1,0:T(8,128)(2,1)}), bf16[16,128,256]{2,1,0:T(8,128)(2,1)S(1)}, u32[]{:S(2)}, u32[]{:S(2)}) async-start(bf16[16,128,256]{2,1,0:T(8,128)(2,1)} %broadcast_in_dim.31), calls=%async_computation.6 | async-start | bytes 2097152 | tf_op jit(solution)/shard_map/all_to_all | solution.py:15
  278.1 23.1 %copy-start = (bf16[64,128,128]{2,1,0:T(8,128)(2,1)S(1)}, bf16[64,128,128]{2,1,0:T(8,128)(2,1)}, u32[]{:S(2)}) copy-start(bf16[64,128,128]{2,1,0:T(8,128)(2,1)} %gather_fusion.2) | copy-start | bytes 6291460
  304.2 39.3 %copy-start.7 = (pred[128,256]{0,1:T(8,128)(4,1)S(1)}, pred[128,256]{0,1:T(8,128)(4,1)}, u32[]{:S(2)}) copy-start(pred[128,256]{0,1:T(8,128)(4,1)} %get-tuple-element.8) | copy-start | bytes 98308
  379.1 36.5 %copy-start.5 = (pred[128,256]{0,1:T(8,128)(4,1)S(1)}, pred[128,256]{0,1:T(8,128)(4,1)}, u32[]{:S(2)}) copy-start(pred[128,256]{0,1:T(8,128)(4,1)} %get-tuple-element.10) | copy-start | bytes 98308
  415.6 0.6 copy-start.3
  451.6 34.9 %copy-start.2 = (f32[128,256]{0,1:T(8,128)S(1)}, f32[128,256]{0,1:T(8,128)}, u32[]{:S(2)}) copy-start(f32[128,256]{0,1:T(8,128)} %copy-done.1) | copy-start | bytes 393220
  451.6 34.8 %copy-start.4 = (f32[128,256]{0,1:T(8,128)S(1)}, f32[128,256]{0,1:T(8,128)}, u32[]{:S(2)}) copy-start(f32[128,256]{0,1:T(8,128)} %copy-done.3) | copy-start | bytes 393220
  451.6 34.8 %copy-start.6 = (pred[128,256]{0,1:T(8,128)(4,1)S(1)}, pred[128,256]{0,1:T(8,128)(4,1)}, u32[]{:S(2)}) copy-start(pred[128,256]{0,1:T(8,128)(4,1)} %get-tuple-element.10) | copy-start | bytes 98308
  451.6 34.8 %copy-start.8 = (pred[128,256]{0,1:T(8,128)(4,1)S(1)}, pred[128,256]{0,1:T(8,128)(4,1)}, u32[]{:S(2)}) copy-start(pred[128,256]{0,1:T(8,128)(4,1)} %get-tuple-element.8) | copy-start | bytes 98308
  451.6 34.8 %copy-start.10 = (pred[128,256]{0,1:T(8,128)(4,1)S(1)}, pred[128,256]{0,1:T(8,128)(4,1)}, u32[]{:S(2)}) copy-start(pred[128,256]{0,1:T(8,128)(4,1)} %get-tuple-element.12) | copy-start | bytes 98308
where the time goes:
time: 489 us; the launch traced here: 487 us
  blocking collectives  322 us (66%)
  waiting for transfers between devices  82.8 us (17%)
  local copies, waits for them, and re-layouts  26.1 us (5%)
  matrix products  21 us (4%)
  starting transfers between devices  19.1 us (4%)
  other arithmetic  15.7 us (3%)
    all_to_all x5, blocking collectives, sent_and_summed(): lax.all_to_all(cut_along(value, dim, devices), axis, 0, 0, tiled=True)  217 us
    all_to_all x4, blocking collectives, from_everyone(): return lax.all_to_all(copies, axis, split_axis=0, concat_axis=0, tiled=True)  105 us
    all_to_all x1, waiting for transfers between devices, sent_and_summed(): lax.all_to_all(cut_along(value, dim, devices), axis, 0, 0, tiled=True)  47.9 us
    all_to_all x2, waiting for transfers between devices, from_everyone(): return lax.all_to_all(copies, axis, split_axis=0, concat_axis=0, tiled=True)  34.8 us
    all_to_all x2, starting transfers between devices, from_everyone(): return lax.all_to_all(copies, axis, split_axis=0, concat_axis=0, tiled=True)  14.5 us
    dot_general x3, matrix products, dest_terms(): jnp.einsum('ibrj,ibjs->irs', tile_values, picked, preferred_element_type=...  11.9 us
  transfers between devices with their start and end apart: 3, of which 3 were waited for; matrix products, arithmetic and copies ran while one was open for 2% of the time, Pallas kernels for 0%

commit v1 on v0

v1 whole, which is shorter than its diff:
```python
import functools

import jax
import jax.numpy as jnp
from jax import lax
from jax.experimental import pallas as pl
from jax.experimental.pallas import tpu as pltpu
from jax.sharding import PartitionSpec as P

MESH = pl.DeviceIdType.MESH
F32, BF16, I16, I32 = jnp.float32, jnp.bfloat16, jnp.int16, jnp.int32

ZS, XS, HI = 8, 4, 2
LVLS = 3
FWD = (-5.0, 1365.0)
BWD = (-44.0, 744.0)
LN2 = 0.6931471805599453
COL_STEPS = [(2, 1), (1, 1), (3, 1), (0, 1), (2, 0), (1, 0), (3, 0)]


def encode(x, code):
    low, steps = code
    v = jnp.log(jnp.maximum(x, 2.0**low)) * (steps / LN2) + (0.5 - low * steps)
    return (v.astype(I32) - 32768).astype(I16)


def decode(c, code):
    low, steps = code
    v = c.astype(I32).astype(F32)
    x = jnp.exp(v * (LN2 / steps) + (32768.0 / steps + low) * LN2)
    return jnp.where(v > -32768.0, x, 0.0)


def kernel(
    tsrc, bslot, paths_in, dep_in, levels, pattern, out,
    stage, acat, at, gath, wgt, local, part, paths, total,
    ysend, yrecv, qsend, qrecv, psend, precv, fsend, frecv,
    csend, crecv, isend, irecv,
    load_sem,
    ag_s, ag_r, sib_s, sib_r,
    y_s, y_r, q_s, q_r, p_s, p_r, f_s, f_r,
    wy_s, wy_r, wb_s, wb_r, wq_s, wq_r, wp_s, wp_r,
    c_s, c_r, i_s, i_r,
):
    r, c = lax.axis_index("row"), lax.axis_index("col")
    z, y = r // 2, r % 2
    chip, core = c // 2, c % 2
    yhi, x = chip // XS, chip % XS
    s = 1 - 2 * core
    half = 64

    def row_dev(zz, yy):
        return {"row": zz * 2 + yy, "col": c}

    def ring(off):
        return (z + s * off + 2 * ZS) % ZS

    ahead, behind = row_dev(ring(1), y), row_dev(ring(-1), y)
    across = row_dev(z, 1 - y)
    sibling = {"row": r, "col": chip * 2 + 1 - core}

    def chip_at(n, sign=1):
        dx, dy = COL_STEPS[n]
        return ((yhi + dy) % HI) * XS + (x + sign * dx + XS) % XS

    def col_dev(n):
        return {"row": r, "col": chip_at(n) * 2 + core}

    def move(src, dst, ssem, rsem, dev):
        return pltpu.make_async_remote_copy(
            src_ref=src, dst_ref=dst, send_sem=ssem, recv_sem=rsem, device_id=dev, device_id_type=MESH
        )

    def load(i):
        return pltpu.make_async_copy(pattern.at[pl.ds(i * 4, 4)], stage.at[i], load_sem.at[i])

    for i in range(16):
        load(i).start()

    barrier = pltpu.get_barrier_semaphore()
    partners = [ahead, behind, across, sibling] + [col_dev(n) for n in range(7)]
    for dev in partners:
        pl.semaphore_signal(barrier, inc=1, device_id=dev, device_id_type=MESH)
    pl.semaphore_wait(barrier, len(partners))

    def gather_col_start(lvl):
        own = gath.at[lvl, c]
        for n in range(7):
            move(own, own, ag_s.at[n], ag_r.at[lvl, n], col_dev(n)).start()
        move(own, own, sib_s.at[7], sib_r.at[lvl, 7], sibling).start()

    def gather_col_end(lvl):
        own = gath.at[lvl, c]
        for n in (5, 6, 4, 3, 1, 2, 0):
            got = gath.at[lvl, chip_at(n, -1) * 2 + core]
            move(got, got, ag_s.at[n], ag_r.at[lvl, n], col_dev(n)).wait_recv()
            move(got, got, sib_s.at[n], sib_r.at[lvl, n], sibling).start()
        for n in range(7):
            move(own, own, ag_s.at[n], ag_r.at[lvl, n], col_dev(n)).wait_send()
        for n in range(8):
            move(own, own, sib_s.at[n], sib_r.at[lvl, n], sibling).wait()

    def zoff(j):
        return jnp.where(j % 2 == 0, 4 - j // 2, (j - 7) // 2)

    def forward_tile(i):
        rhs = jnp.concatenate([local[tsrc[i * 4 + e]] for e in range(4)], axis=0)
        part[i] = jnp.dot(acat[i], rhs, preferred_element_type=F32)

    def y_move(lvl, j):
        return move(ysend.at[j], yrecv.at[lvl, j], y_s.at[j], y_r.at[lvl, j], across)

    def q_move(lvl, m, dev):
        return move(qsend.at[m], qrecv.at[lvl, m], q_s.at[m], q_r.at[lvl, m], dev)

    def p_move(lvl, m, dev):
        return move(psend.at[m], precv.at[lvl, m], p_s.at[m], p_r.at[lvl, m], dev)

    def forward_pair(lvl, j):
        zd = ring(zoff(j))

        @pl.loop(0, 2)
        def _(t):
            forward_tile(zd * 2 + t)

        ysend[j] = encode(part[zd * 2 + 1 - y, :half], FWD)
        y_move(lvl, j).start()

    def q_sum(lvl, j, got):
        zd = ring(zoff(j))
        for t in range(2):
            v = part[zd * 2 + t, half:]
            for m in got:
                v += decode(qrecv[lvl, m, t], FWD)
            yield t, v

    def p_sum(lvl, j, got):
        y_move(lvl, j).wait_recv()
        v = part[ring(zoff(j)) * 2 + y, :half] + decode(yrecv[lvl, j], FWD)
        for m in got:
            v += decode(precv[lvl, m], FWD)
        return v

    def hop(m):
        return (2 * m, ahead) if m < 4 else (2 * (m - 4) + 1, behind)

    def q_step(lvl, m):
        j, dev = hop(m)
        got = [] if m in (0, 4) else [m - 1]
        for g in got:
            q_move(lvl, g, dev).wait_recv()
        for t, v in q_sum(lvl, j, got):
            qsend[m, t] = encode(v, FWD)
        q_move(lvl, m, dev).start()

    def p_step(lvl, m):
        j, dev = hop(m)
        got = [] if m in (0, 4) else [m - 1]
        for g in got:
            p_move(lvl, g, dev).wait_recv()
        psend[m] = encode(p_sum(lvl, j, got), FWD)
        p_move(lvl, m, dev).start()

    def f_move(lvl):
        return move(fsend, frecv.at[lvl], f_s, f_r.at[lvl], across)

    def sum_row(lvl):
        @pl.loop(0, 2)
        def _(j):
            forward_pair(lvl, j)

        q_step(lvl, 0)
        q_step(lvl, 4)

        @pl.loop(2, 4)
        def _(j):
            forward_pair(lvl, j)

        p_step(lvl, 0)
        p_step(lvl, 4)

        @pl.loop(4, 8)
        def _(j):
            forward_pair(lvl, j)

        for m in (1, 5, 2, 6, 3):
            q_step(lvl, m)
            p_step(lvl, m)
        for m in (3, 6):
            q_move(lvl, m, ahead).wait_recv()
        for t, v in q_sum(lvl, 7, [3, 6]):
            part[z * 2 + t, half:] = v
        fsend[...] = encode(part[z * 2 + 1 - y, half:], FWD)
        f_move(lvl).start()
        for m in (3, 6):
            p_move(lvl, m, ahead).wait_recv()
        total[:half] = p_sum(lvl, 7, [3, 6])
        f_move(lvl).wait()
        total[half:] = part[z * 2 + y, half:] + decode(frecv[lvl], FWD)
        for j in range(8):
            y_move(lvl, j).wait_send()
        for m in range(7):
            q_move(lvl, m, ahead).wait_send()
            p_move(lvl, m, ahead).wait_send()

    def came_from(m):
        return ring(-(m + 1)) if m < 4 else ring(m - 3)

    def wb_move(lvl, zz, m, dev):
        ref = wgt.at[lvl, zz * 2 + y]
        return move(ref, ref, wb_s.at[m], wb_r.at[lvl, m], dev)

    def wq_move(lvl, zz, m, dev):
        ref = wgt.at[lvl, zz * 2 + 1 - y, pl.ds(half, half)]
        return move(ref, ref, wq_s.at[m], wq_r.at[lvl, m], dev)

    def wp_move(lvl, zz, m):
        ref = wgt.at[lvl, zz * 2 + y, pl.ds(0, half)]
        return move(ref, ref, wp_s.at[m], wp_r.at[lvl, m], across)

    def wy_move(lvl):
        ref = wgt.at[lvl, r]
        return move(ref, ref, wy_s, wy_r.at[lvl], across)

    def gather_row(lvl):
        wy_move(lvl).start()
        wb_move(lvl, z, 0, ahead).start()
        wb_move(lvl, z, 4, behind).start()
        wy_move(lvl).wait_recv()
        wq_move(lvl, z, 0, ahead).start()
        wq_move(lvl, z, 4, behind).start()
        for m in (0, 4, 1, 5, 2, 6, 3):
            dev = ahead if m < 4 else behind
            zz = came_from(m)
            wb_move(lvl, zz, m, dev).wait_recv()
            if m not in (3, 6):
                wb_move(lvl, zz, m + 1, dev).start()
            wp_move(lvl, zz, m).start()
            wq_move(lvl, zz, m, dev).wait_recv()
            if m not in (3, 6):
                wq_move(lvl, zz, m + 1, dev).start()
        wy_move(lvl).wait_send()
        for m in range(7):
            wb_move(lvl, z, m, ahead).wait_send()
            wq_move(lvl, z, m, ahead).wait_send()
            wp_move(lvl, z, m).wait()

    def back_tile(t):
        slots = [bslot[t * 4 + e] for e in range(4)]
        lhs = jnp.concatenate([at[k] for k in slots], axis=1)
        rhs = jnp.concatenate([local[k // 4] for k in slots], axis=0)
        part[t] = jnp.dot(lhs, rhs, preferred_element_type=F32)

    def c_move(lvl, n):
        return move(csend.at[n], crecv.at[lvl, n], c_s.at[n], c_r.at[lvl, n], sibling)

    def i_move(lvl, n):
        return move(isend.at[n], irecv.at[lvl, n], i_s.at[n], i_r.at[lvl, n], col_dev(n))

    def dest_chip(n):
        return chip if n == 7 else chip_at(n)

    def sum_col(lvl):
        for n in range(8):
            t = dest_chip(n) * 2 + 1 - core
            back_tile(t)
            csend[n] = encode(part[t], BWD)
            c_move(lvl, n).start()
        for n in range(8):
            t = dest_chip(n) * 2 + core
            back_tile(t)
            c_move(lvl, n).wait_recv()
            v = part[t] + decode(crecv[lvl, n], BWD)
            if n < 7:
                isend[n] = encode(v, BWD)
                i_move(lvl, n).start()
            else:
                total[...] = v
        for n in (5, 6, 4, 3, 1, 2, 0):
            i_move(lvl, n).wait_recv()
            total[...] += decode(irecv[lvl, n], BWD)
        for n in range(8):
            c_move(lvl, n).wait_send()
        for n in range(7):
            i_move(lvl, n).wait_send()

    first = jnp.where(levels[...] == 0, paths_in[...], 0.0)
    paths[0] = first
    gath[0, c] = first.astype(BF16)
    gather_col_start(0)

    eye = (
        lax.broadcasted_iota(I32, (128, 128), 0) == lax.broadcasted_iota(I32, (128, 128), 1)
    ).astype(F32).astype(BF16)
    for i in range(16):
        load(i).wait()

    @pl.loop(0, 16)
    def _(i):
        for e in range(4):
            tile = stage[i, e].astype(F32).astype(BF16)
            acat[i, :, e * 128 : (e + 1) * 128] = tile
            at[i * 4 + e] = lax.dot_general(
                eye, tile, (((1,), (1,)), ((), ())), preferred_element_type=F32
            ).astype(BF16)

    @pl.loop(0, LVLS)
    def _(lvl):
        gather_col_end(lvl)
        local[...] = gath[lvl]
        sum_row(lvl)
        level = lvl + 1
        now = jnp.where(levels[...] == level, total[...], 0.0)
        paths[level] = now

        @pl.when(lvl < LVLS - 1)
        def _():
            gath[level, c] = now.astype(BF16)
            gather_col_start(level)

    weight = jnp.where(levels[...] == 3, 1.0 + dep_in[...], 0.0) / jnp.maximum(paths[3], 1.0)
    wgt[0, r] = weight.astype(BF16)
    out[...] = jnp.zeros_like(out)

    @pl.loop(0, LVLS)
    def _(lvl):
        gather_row(lvl)
        local[...] = wgt[lvl]
        sum_col(lvl)
        level = 2 - lvl
        mask = levels[...] == level
        delta = jnp.where(mask, paths[level] * total[...], 0.0)
        out[...] += delta

        @pl.when(lvl < LVLS - 1)
        def _():
            weight = jnp.where(mask, 1.0 + delta, 0.0) / jnp.maximum(paths[level], 1.0)
            wgt[lvl + 1, r] = weight.astype(BF16)


def slots_by_source(flat, tiles, per):
    eq = (flat[None, :] == jnp.arange(tiles, dtype=I32)[:, None]).astype(I32)
    slot = jnp.arange(flat.shape[0], dtype=I32)
    before = jnp.sum(
        jnp.where((flat[:, None] == flat[None, :]) & (slot[:, None] < slot[None, :]), 1, 0), axis=0
    )
    picked = eq[:, None, :] * (before[None, None, :] == jnp.arange(per, dtype=I32)[None, :, None])
    return jnp.sum(picked * slot[None, None, :], axis=2).reshape(-1)


def shards(paths_in, dep_in, levels, tile_src, pattern):
    rows, sources = paths_in.shape
    flat = tile_src.reshape(-1)
    tiles, half = 16, rows // 2
    back = slots_by_source(flat, tiles, 4)
    pattern = pattern.reshape(64, 128, 128)
    vmem, smem = pl.BlockSpec(memory_space=pltpu.VMEM), pl.BlockSpec(memory_space=pltpu.SMEM)
    dma = pltpu.SemaphoreType.DMA
    block = (rows, sources)
    halfb = (half, sources)
    return pl.pallas_call(
        kernel,
        out_shape=jax.ShapeDtypeStruct(block, F32),
        in_specs=[smem, smem, vmem, vmem, vmem, pl.BlockSpec(memory_space=pl.ANY)],
        out_specs=vmem,
        scratch_shapes=[
            pltpu.VMEM((16, 4, 128, 128), I32),
            pltpu.VMEM((16, 128, 512), BF16),
            pltpu.VMEM((64, 128, 128), BF16),
            pltpu.VMEM((LVLS, tiles, *block), BF16),
            pltpu.VMEM((LVLS, tiles, *block), BF16),
            pltpu.VMEM((tiles, *block), BF16),
            pltpu.VMEM((tiles, *block), F32),
            pltpu.VMEM((4, *block), F32),
            pltpu.VMEM(block, F32),
            pltpu.VMEM((8, *halfb), I16),
            pltpu.VMEM((LVLS, 8, *halfb), I16),
            pltpu.VMEM((7, 2, *halfb), I16),
            pltpu.VMEM((LVLS, 7, 2, *halfb), I16),
            pltpu.VMEM((7, *halfb), I16),
            pltpu.VMEM((LVLS, 7, *halfb), I16),
            pltpu.VMEM(halfb, I16),
            pltpu.VMEM((LVLS, *halfb), I16),
            pltpu.VMEM((8, *block), I16),
            pltpu.VMEM((LVLS, 8, *block), I16),
            pltpu.VMEM((7, *block), I16),
            pltpu.VMEM((LVLS, 7, *block), I16),
            dma((16,)),
            dma((7,)), dma((LVLS, 7)), dma((8,)), dma((LVLS, 8)),
            dma((8,)), dma((LVLS, 8)), dma((7,)), dma((LVLS, 7)), dma((7,)), dma((LVLS, 7)), dma, dma((LVLS,)),
            dma, dma((LVLS,)), dma((7,)), dma((LVLS, 7)), dma((7,)), dma((LVLS, 7)), dma((7,)), dma((LVLS, 7)),
            dma((8,)), dma((LVLS, 8)), dma((7,)), dma((LVLS, 7)),
        ],
        compiler_params=pltpu.CompilerParams(
            collective_id=0, has_side_effects=True, vmem_limit_bytes=48 * 1024 * 1024
        ),
    )(flat, back, paths_in, dep_in, levels, pattern)


def solution(mesh):
    placed = (
        P(("row", "col"), None),
        P(("row", "col"), None),
        P(("row", "col"), None),
        P("row", "col", None, None),
        P("row", "col", None, None, None, None),
    )
    return jax.shard_map(
        shards, mesh=mesh, in_specs=placed, out_specs=P(("row", "col"), None), check_vma=False
    )
```

time: 489 us -> 194 us (0.40)
  blocking collectives: 322 us -> 0 us
  Pallas kernels: 0 us -> 187 us
  waiting for transfers between devices: 82.8 us -> 0 us
  matrix products: 21 us -> 0 us
  local copies, waits for them, and re-layouts: 26.1 us -> 6.58 us
  starting transfers between devices: 19.1 us -> 0 us
  other arithmetic: 15.7 us -> 0.25 us
    all_to_all x9 -> x0, blocking collectives: 322 us -> none  [the longest x5 217 us: sent_and_summed(): lax.all_to_all(cut_along(value, dim, devices), axis, 0, 0, tiled=True)]
    pallas_call x0 -> x1, Pallas kernels: none -> 187 us  [shards(): pl.pallas_call(kernel, out_shape=jax.ShapeDtypeStruct(block, F32), in_spe...]
    all_to_all x3 -> x0, waiting for transfers between devices: 82.8 us -> none  [the longest x1 47.9 us: sent_and_summed(): lax.all_to_all(cut_along(value, dim, devices), axis, 0, 0, tiled=True)]
    dot_general x6 -> x0, matrix products: 21 us -> none  [the longest x3 11.9 us: dest_terms(): jnp.einsum('ibrj,ibjs->irs', tile_values, picked, preferred_element_type=...]
    all_to_all x3 -> x0, starting transfers between devices: 19.1 us -> none  [the longest x2 14.5 us: from_everyone(): return lax.all_to_all(copies, axis, split_axis=0, concat_axis=0, tiled=True)]
    gather x7 -> x0, local copies, waits for them, and re-layouts: 18.6 us -> none  [the longest x3 8.22 us: dest_terms(): picked = pieces[source_ids]]
    reduce_sum x6 -> x2, other arithmetic: 8.69 us -> 0.24 us  [the longest x1 0.14 us: slots_by_source(): return jnp.sum(picked * slot[None, None, :], axis=2).reshape(-1)]
  transfers between devices with their start and end apart: 3 -> 0, of which waited for: 3 -> 0; matrix products, arithmetic and copies ran while one was open for 2% -> 0% of each run, Pallas kernels for 0% -> 0%
where the time goes in v1:
time: 194 us
  Pallas kernels  187 us (96%)
  local copies, waits for them, and re-layouts  6.58 us (3%)
    pallas_call x1, Pallas kernels, shards(): pl.pallas_call(kernel, out_shape=jax.ShapeDtypeStruct(block, F32), in_spe...  187 us
    unnamed x10, local copies, waits for them, and re-layouts  6.31 us

profile of v1, /device:TPU:1, one launch (start us, length us, event | category | flops | bytes accessed | tf_op | source)
XLA Modules:
  0.0 194.0 jit_solution(11136464324792287882)
XLA Ops:
  0.0 0.8 copy.8
  0.8 0.1 reshape.58.tsrc
  0.8 0.1 select_reduce_fusion
  1.0 0.1 multiply_reduce_fusion
  1.1 0.1 copy.9
  1.2 0.1 reshape.59.bslot
  1.3 0.0 copy-start
  1.3 2.2 %copy-done = s32[1,1,16,4,128,128]{5,4,3,2,1,0:T(8,128)S(1)} copy-done((s32[1,1,16,4,128,128]{5,4,3,2,1,0:T(8,128)S(1)}, s32[1,1,16,4,128,128]{5,4,3,2,1,0:T(8,128)}, u32[]{:S(2)}) %copy-start) | copy-done | bytes 4194328
  3.5 0.0 copy-start.1
  3.5 0.9 copy-done.1
  4.4 0.0 copy-start.2
  4.4 0.9 copy-done.2
  5.3 0.0 copy-start.3
  5.3 0.9 copy-done.3
  6.2 187.2 %shard_map.55 = f32[128,256]{1,0:T(8,128)S(1)} custom-call(s32[64]{0:T(128)S(1)} %reshape.58.tsrc, s32[64]{0:T(128)S(1)} %reshape.59.bslot, f32[128,256]{1,0:T(8,128)S(1)} %copy-done.1, f32[128,256]{1,0:T(8,128)S(1)} %copy-done.2, s32[128,256]{1,0:T(8,128)S(1)} %copy-done.3, s32[64,128,128]{2,1,0:T(8,128)S(1)} %bitcast.3), custom_call_target="tpu_custom_call" | custom-call | tf_op jit(solution)/shard_map/pallas_call | solution.py:361
  193.4 0.7 copy.11
  (2 shorter events, 0.0 us)
Async XLA Ops:
  1.3 2.2 %copy-start = (s32[1,1,16,4,128,128]{5,4,3,2,1,0:T(8,128)S(1)}, s32[1,1,16,4,128,128]{5,4,3,2,1,0:T(8,128)}, u32[]{:S(2)}) copy-start(s32[1,1,16,4,128,128]{5,4,3,2,1,0:T(8,128)} %param.9) | copy-start | bytes 12582916
  3.5 0.9 copy-start.1
  4.4 0.9 copy-start.2
  5.3 0.9 copy-start.3

commit v2 on v0

v2 whole, which is shorter than its diff:
```python
import jax
import jax.numpy as jnp
from jax import lax
from jax.experimental import pallas as pl
from jax.experimental.pallas import tpu as pltpu
from jax.sharding import PartitionSpec as P

MESH = pl.DeviceIdType.MESH
F32, BF16, I16, I32 = jnp.float32, jnp.bfloat16, jnp.int16, jnp.int32

ZS, XS, HI = 8, 4, 2
TILE, BAND, TILES = 128, 4, 16
LVLS = 3
NB = 1
PR = 80
QR = TILE - PR
FWD = (-5.0, 1365.0)
BWD = (-44.0, 744.0)
LN2 = 0.6931471805599453


def encode(x, code):
    low, steps = code
    v = jnp.log(jnp.maximum(x, 2.0**low)) * (steps / LN2) + (0.5 - low * steps)
    return (v.astype(I32) - 32768).astype(I16)


def decode(c, code):
    low, steps = code
    v = c.astype(I32).astype(F32)
    x = jnp.exp(v * (LN2 / steps) + (32768.0 / steps + low) * LN2)
    return jnp.where(v > -32768.0, x, 0.0)


def kernel(
    tsrc, bslot, paths_hbm, dep_hbm, levels_hbm, pattern, out,
    paths_in, dep_in, levels,
    stage, acat, at, gath, wgt, local, part, paths, total,
    ysend, yrecv, zsend, zrecv, qsend, qrecv, fsend, frecv, csend, crecv, isend, irecv,
    load_sem, in_sem,
    ag_s, ag_r, sib_s, sib_r, y_s, y_r, z_s, z_r, q_s, q_r, f_s, f_r,
    wz_s, wz_r, wy_s, wy_r, wq_s, wq_r, wf_s, wf_r, c_s, c_r, i_s, i_r,
):
    r, c = lax.axis_index("row"), lax.axis_index("col")
    z, y = r // 2, r % 2
    chip, core = c // 2, c % 2
    yhi, x = chip // XS, chip % XS
    lanes = gath.shape[-1]

    def load(i):
        return pltpu.make_async_copy(pattern.at[pl.ds(i * BAND, BAND)], stage.at[i], load_sem.at[i])

    inputs = [
        pltpu.make_async_copy(src, dst, in_sem.at[n])
        for n, (src, dst) in enumerate(
            [(paths_hbm, paths_in), (levels_hbm, levels), (dep_hbm, dep_in)]
        )
    ]
    for copy in inputs:
        copy.start()
    for i in range(TILES):
        load(i).start()

    def z_off(j):
        return (1 - 2 * core) * jnp.where(j % 2 == 1, (7 - j) // 2, -((8 - j) // 2))

    def z_to(j):
        return (z + z_off(j) + ZS) % ZS

    def c_to(n, sign=1):
        dx, dy = (7 - n) % XS, (7 - n) // XS
        return ((yhi + dy) % HI) * XS + (x + sign * dx + XS) % XS

    def z_dev(hops):
        return {"row": z_hop(hops) * 2 + y, "col": c}

    def z_hop(hops):
        return (z + (1 - 2 * core) * hops + ZS) % ZS

    def c_dev(n):
        return {"row": r, "col": c_to(n) * 2 + core}

    across = {"row": z * 2 + 1 - y, "col": c}
    sibling = {"row": r, "col": chip * 2 + 1 - core}

    def move(src, dst, ssem, rsem, dev):
        return pltpu.make_async_remote_copy(
            src_ref=src, dst_ref=dst, send_sem=ssem, recv_sem=rsem, device_id=dev, device_id_type=MESH
        )

    barrier = pltpu.get_barrier_semaphore()
    partners = [across, sibling] + [z_dev(hops) for hops in (2, 1, -1, -2)] + [c_dev(n) for n in range(7)]
    for dev in partners:
        pl.semaphore_signal(barrier, inc=1, device_id=dev, device_id_type=MESH)
    pl.semaphore_wait(barrier, len(partners))

    def ag_move(b, lvl, n, place):
        ref = gath.at[b, lvl, place]
        return move(ref, ref, ag_s.at[b, n], ag_r.at[b, lvl, n], c_dev(n))

    def sib_move(b, lvl, n, place):
        ref = gath.at[b, lvl, place]
        return move(ref, ref, sib_s.at[b, n], sib_r.at[b, lvl, n], sibling)

    def y_move(b, lvl, j):
        return move(ysend.at[b, j], yrecv.at[b, lvl, j], y_s.at[b, j], y_r.at[b, lvl, j], across)

    def hop_dev(j):
        return z_dev((2, 1, -1, 2, -2, 1, -1)[j])

    def z_move(b, lvl, j):
        return move(zsend.at[b, j], zrecv.at[b, lvl, j], z_s.at[b, j], z_r.at[b, lvl, j], hop_dev(j))

    def q_move(b, lvl, j):
        return move(qsend.at[b, j], qrecv.at[b, lvl, j], q_s.at[b, j], q_r.at[b, lvl, j], hop_dev(j))

    def f_move(b, lvl):
        return move(fsend.at[b, 0], frecv.at[b, lvl, 0], f_s.at[b, 0], f_r.at[b, lvl, 0], across)

    def z_go(b, lvl, j):
        y_move(b, lvl, j).wait_recv()
        v = part[b, 0, j, :PR] + decode(yrecv[b, lvl, j], FWD)
        for m in {3: (1, 0), 4: (2,)}.get(j, ()):
            z_move(b, lvl, m).wait_recv()
            v += decode(zrecv[b, lvl, m], FWD)
        zsend[b, j] = encode(v, FWD)
        z_move(b, lvl, j).start()

    def q_go(b, lvl, j):
        joined = {3: (1, 0), 4: (2,)}.get(j, ())
        for m in joined:
            q_move(b, lvl, m).wait_recv()
        for k in range(2):
            v = part[b, k, j, PR:]
            for m in joined:
                v += decode(qrecv[b, lvl, m, k], FWD)
            qsend[b, j, k] = encode(v, FWD)
        q_move(b, lvl, j).start()

    def fwd_send(b, lvl, value):
        gath[b, lvl, c] = value.astype(BF16)
        for n in range(7):
            ag_move(b, lvl, n, c).start()
        sib_move(b, lvl, 7, c).start()

    def fwd_pass(b, lvl):
        for n in (6, 4, 5, 3, 2, 0, 1):
            place = c_to(n, -1) * 2 + core
            ag_move(b, lvl, n, place).wait_recv()
            sib_move(b, lvl, n, place).start()

    def fwd_tile(b, i):
        rhs = jnp.concatenate([local[b, tsrc[e, i]] for e in range(BAND)], axis=0)
        return jnp.dot(acat[i], rhs, preferred_element_type=F32)

    def fwd_work(b, lvl):
        for n in range(8):
            sib_move(b, lvl, n, c).wait_recv()
        local[b] = gath[b, lvl]

        def pair(j):
            for k, i in ((1, z_to(j) * 2 + 1 - y), (0, z_to(j) * 2 + y)):
                part[b, k, j] = fwd_tile(b, i)
            ysend[b, j] = encode(part[b, 1, j, :PR], FWD)
            y_move(b, lvl, j).start()

        for j in range(3):
            pair(j)
            q_go(b, lvl, j)

        for j in (5, 6, 3, 4, 7):
            pair(j)
            if j == 6:
                q_go(b, lvl, 5)
                q_go(b, lvl, 6)

    def fwd_mid(b, lvl):
        for j in (0, 1, 2):
            z_go(b, lvl, j)
        for j in (3, 4):
            q_go(b, lvl, j)
        for j in (5, 6, 3, 4):
            z_go(b, lvl, j)

    def fwd_end(b, lvl):
        own = part[b, 0, 7, PR:]
        other = part[b, 1, 7, PR:]
        for j in (6, 5, 4, 3):
            q_move(b, lvl, j).wait_recv()
            own += decode(qrecv[b, lvl, j, 0], FWD)
            other += decode(qrecv[b, lvl, j, 1], FWD)
        fsend[b, 0] = encode(other, FWD)
        f_move(b, lvl).start()
        y_move(b, lvl, 7).wait_recv()
        mine = part[b, 0, 7, :PR] + decode(yrecv[b, lvl, 7], FWD)
        for j in (6, 5, 4, 3):
            z_move(b, lvl, j).wait_recv()
            mine += decode(zrecv[b, lvl, j], FWD)
        total[b, :PR] = mine
        f_move(b, lvl).wait()
        total[b, PR:] = own + decode(frecv[b, lvl, 0], FWD)
        for j in range(7):
            q_move(b, lvl, j).wait_send()
        for n in range(7):
            ag_move(b, lvl, n, c).wait_send()
            z_move(b, lvl, n).wait_send()
        for n in range(8):
            sib_move(b, lvl, n, c).wait_send()
            y_move(b, lvl, n).wait_send()
        level = lvl + 1
        value = jnp.where(levels_of(b) == level, total[b], 0.0)
        paths[b, level] = value
        return value

    def relay_dev(j):
        return z_dev((2, -2, 1, -1, 2, 1, -1)[j])

    def origin(j):
        return z_hop((-2, 2, -1, 1, -4, -3, 3)[j])

    def wz_move(b, lvl, j, zz):
        ref = wgt.at[b, lvl, zz * 2 + y]
        return move(ref, ref, wz_s.at[b, j], wz_r.at[b, lvl, j], relay_dev(j))

    def wq_move(b, lvl, j, zz):
        ref = wgt.at[b, lvl, zz * 2 + 1 - y, pl.ds(PR, QR)]
        return move(ref, ref, wq_s.at[b, j], wq_r.at[b, lvl, j], relay_dev(j))

    def wy_move(b, lvl, j, zz):
        ref = wgt.at[b, lvl, zz * 2 + y, pl.ds(0, PR)]
        return move(ref, ref, wy_s.at[b, j], wy_r.at[b, lvl, j], across)

    def wf_move(b, lvl):
        ref = wgt.at[b, lvl, r, pl.ds(PR, QR)]
        return move(ref, ref, wf_s.at[b, 0], wf_r.at[b, lvl, 0], across)

    def c_move(b, lvl, n):
        return move(csend.at[b, n], crecv.at[b, lvl, n], c_s.at[b, n], c_r.at[b, lvl, n], sibling)

    def i_move(b, lvl, n):
        return move(isend.at[b, n], irecv.at[b, lvl, n], i_s.at[b, n], i_r.at[b, lvl, n], c_dev(n))

    def bwd_send(b, lvl, value):
        wgt[b, lvl, r] = value.astype(BF16)
        wf_move(b, lvl).start()
        for j in range(4):
            wz_move(b, lvl, j, z).start()
        wy_move(b, lvl, 7, z).start()

    def bwd_pass(b, lvl):
        wf_move(b, lvl).wait_recv()
        for j in range(4):
            wq_move(b, lvl, j, z).start()
        def take(go, j):
            go(b, lvl, j, origin(j)).wait_recv()
            for m in {0: (4, 5), 1: (6,)}.get(j, ()):
                go(b, lvl, m, origin(j)).start()
            if go is wz_move:
                wy_move(b, lvl, j, origin(j)).start()

        for j in (2, 3, 0, 1):
            take(wz_move, j)
        take(wq_move, 0)
        take(wq_move, 1)
        for j in (5, 6, 4):
            take(wz_move, j)
        for j in (2, 3, 5, 6, 4):
            take(wq_move, j)

    def bwd_tile(b, t):
        slots = [bslot[t * BAND + e] for e in range(BAND)]
        lhs = jnp.concatenate([at[k] for k in slots], axis=1)
        rhs = jnp.concatenate([local[b, k % TILES] for k in slots], axis=0)
        return jnp.dot(lhs, rhs, preferred_element_type=F32)

    def bwd_work(b, lvl):
        for j in range(8):
            wy_move(b, lvl, j, z).wait_recv()
        local[b] = wgt[b, lvl]

        @pl.loop(0, 8)
        def _(n):
            csend[b, n] = encode(bwd_tile(b, c_to(n) * 2 + 1 - core), BWD)
            c_move(b, lvl, n).start()

        @pl.loop(0, 8)
        def _(n):
            part[b, 0, n] = bwd_tile(b, c_to(n) * 2 + core)

    def bwd_mid(b, lvl):
        for n in range(7):
            c_move(b, lvl, n).wait_recv()
            v = part[b, 0, n] + decode(crecv[b, lvl, n], BWD)
            isend[b, n] = encode(v, BWD)
            i_move(b, lvl, n).start()

        c_move(b, lvl, 7).wait_recv()
        total[b] = part[b, 0, 7] + decode(crecv[b, lvl, 7], BWD)

    def bwd_end(b, lvl):
        for n in (6, 4, 5, 3, 2, 0, 1):
            i_move(b, lvl, n).wait_recv()
            total[b] += decode(irecv[b, lvl, n], BWD)
        for n in range(7):
            wz_move(b, lvl, n, z).wait_send()
            wq_move(b, lvl, n, z).wait_send()
            i_move(b, lvl, n).wait_send()
        for n in range(8):
            wy_move(b, lvl, n, z).wait_send()
            c_move(b, lvl, n).wait_send()
        wf_move(b, lvl).wait_send()
        level = 2 - lvl
        mask = levels_of(b) == level
        delta = jnp.where(mask, paths[b, level] * total[b], 0.0)
        out[:, b * lanes : (b + 1) * lanes] += delta
        return jnp.where(mask, 1.0 + delta, 0.0) / jnp.maximum(paths[b, level], 1.0)

    def levels_of(b):
        return levels[:, b * lanes : (b + 1) * lanes]

    def fwd_next(b, lvl):
        value = fwd_end(b, lvl)

        @pl.when(lvl < LVLS - 1)
        def _():
            fwd_send(b, lvl + 1, value)

        @pl.when(lvl == LVLS - 1)
        def _():
            turn(b, value)

    def turn(b, value):
        top = jnp.where(levels_of(b) == 3, 1.0 + dep_in[:, b * lanes : (b + 1) * lanes], 0.0)
        bwd_send(b, 0, top / jnp.maximum(value, 1.0))

    def bwd_next(b, lvl):
        value = bwd_end(b, lvl)

        @pl.when(lvl < LVLS - 1)
        def _():
            bwd_send(b, lvl + 1, value)

    inputs[0].wait()
    inputs[1].wait()
    for b in range(NB):
        value = jnp.where(levels_of(b) == 0, paths_in[:, b * lanes : (b + 1) * lanes], 0.0)
        paths[b, 0] = value
        fwd_send(b, 0, value)
    inputs[2].wait()
    out[...] = jnp.zeros_like(out)

    eye = (
        lax.broadcasted_iota(I32, (TILE, TILE), 0) == lax.broadcasted_iota(I32, (TILE, TILE), 1)
    ).astype(F32).astype(BF16)
    for i in range(TILES):
        load(i).wait()

    @pl.loop(0, TILES)
    def _(i):
        for e in range(BAND):
            tile = stage[i, e].astype(F32).astype(BF16)
            acat[i, :, e * TILE : (e + 1) * TILE] = tile
            at[e * TILES + i] = lax.dot_general(
                eye, tile, (((1,), (1,)), ((), ())), preferred_element_type=F32
            ).astype(BF16)

    batches = range(NB)

    def each(*stages):
        def body(lvl):
            for stage in stages:
                for b in batches:
                    stage(b, lvl)

        return body

    pl.loop(0, LVLS)(each(fwd_pass, fwd_work, fwd_mid, fwd_next))
    pl.loop(0, LVLS)(each(bwd_pass, bwd_work, bwd_mid, bwd_next))


def slots_by_source(flat):
    slots = jnp.arange(TILES * BAND, dtype=I32)
    same = (flat[:, None] == flat[None, :]) & (slots[:, None] < slots[None, :])
    before = jnp.sum(same.astype(I32), axis=0)
    mine = flat[None, :] == jnp.arange(TILES, dtype=I32)[:, None]
    nth = before[None, :] == jnp.arange(BAND, dtype=I32)[:, None]
    picked = mine[:, None, :] & nth[None, :, :]
    return jnp.sum(jnp.where(picked, slots, 0), axis=2).reshape(-1)


def shards(paths_in, dep_in, levels, tile_src, pattern):
    rows, sources = paths_in.shape
    by_slot = tile_src[0, 0].T
    back = slots_by_source(by_slot.reshape(-1))
    pattern = pattern.reshape(TILES * BAND, TILE, TILE)
    vmem, smem, hbm = (
        pl.BlockSpec(memory_space=m) for m in (pltpu.VMEM, pltpu.SMEM, pltpu.HBM)
    )
    block = (rows, sources // NB)
    whole = (rows, sources)

    def dma(*shape):
        return pltpu.SemaphoreType.DMA(shape)

    def pairs(*counts):
        return [d for n in counts for d in (dma(NB, n), dma(NB, LVLS, n))]

    def slots(*dims):
        shape = (*dims, sources // NB)
        return [pltpu.VMEM((NB, *shape), I16), pltpu.VMEM((NB, LVLS, *shape), I16)]

    return pl.pallas_call(
        kernel,
        out_shape=jax.ShapeDtypeStruct(whole, F32),
        in_specs=[smem, smem, hbm, hbm, hbm, hbm],
        out_specs=vmem,
        scratch_shapes=[
            pltpu.VMEM(whole, F32),
            pltpu.VMEM(whole, F32),
            pltpu.VMEM(whole, I32),
            pltpu.VMEM((TILES, BAND, TILE, TILE), I32),
            pltpu.VMEM((TILES, TILE, BAND * TILE), BF16),
            pltpu.VMEM((TILES * BAND, TILE, TILE), BF16),
            pltpu.VMEM((NB, LVLS, TILES, *block), BF16),
            pltpu.VMEM((NB, LVLS, TILES, *block), BF16),
            pltpu.VMEM((NB, TILES, *block), BF16),
            pltpu.VMEM((NB, 2, 8, *block), F32),
            pltpu.VMEM((NB, 4, *block), F32),
            pltpu.VMEM((NB, *block), F32),
            *slots(8, PR), *slots(7, PR), *slots(7, 2, QR), *slots(1, QR), *slots(8, rows), *slots(7, rows),
            dma(TILES),
            dma(3),
            *pairs(7, 8, 8, 7, 7, 1),
            *pairs(7, 8, 7, 1, 8, 7),
        ],
        compiler_params=pltpu.CompilerParams(
            collective_id=0, has_side_effects=True, vmem_limit_bytes=56 * 1024 * 1024
        ),
    )(by_slot, back, paths_in, dep_in, levels, pattern)


def solution(mesh):
    placed = (
        P(("row", "col"), None),
        P(("row", "col"), None),
        P(("row", "col"), None),
        P("row", "col", None, None),
        P("row", "col", None, None, None, None),
    )
    return jax.shard_map(
        shards, mesh=mesh, in_specs=placed, out_specs=P(("row", "col"), None), check_vma=False
    )
```

time: 489 us -> 165 us (0.34)
  blocking collectives: 322 us -> 0 us
  Pallas kernels: 0 us -> 160 us
  waiting for transfers between devices: 82.8 us -> 0 us
  local copies, waits for them, and re-layouts: 26.1 us -> 3.02 us
  matrix products: 21 us -> 0 us
  starting transfers between devices: 19.1 us -> 0 us
  other arithmetic: 15.7 us -> 0.26 us
    all_to_all x9 -> x0, blocking collectives: 322 us -> none  [the longest x5 217 us: sent_and_summed(): lax.all_to_all(cut_along(value, dim, devices), axis, 0, 0, tiled=True)]
    pallas_call x0 -> x1, Pallas kernels: none -> 160 us  [shards(): pl.pallas_call(kernel, out_shape=jax.ShapeDtypeStruct(whole, F32), in_spe...]
    all_to_all x3 -> x0, waiting for transfers between devices: 82.8 us -> none  [the longest x1 47.9 us: sent_and_summed(): lax.all_to_all(cut_along(value, dim, devices), axis, 0, 0, tiled=True)]
    dot_general x6 -> x0, matrix products: 21 us -> none  [the longest x3 11.9 us: dest_terms(): jnp.einsum('ibrj,ibjs->irs', tile_values, picked, preferred_element_type=...]
    all_to_all x3 -> x0, starting transfers between devices: 19.1 us -> none  [the longest x2 14.5 us: from_everyone(): return lax.all_to_all(copies, axis, split_axis=0, concat_axis=0, tiled=True)]
    gather x7 -> x0, local copies, waits for them, and re-layouts: 18.6 us -> none  [the longest x3 8.22 us: dest_terms(): picked = pieces[source_ids]]
    reduce_sum x6 -> x2, other arithmetic: 8.69 us -> 0.25 us  [the longest x1 0.15 us: slots_by_source(): return jnp.sum(jnp.where(picked, slots, 0), axis=2).reshape(-1)]
  transfers between devices with their start and end apart: 3 -> 0, of which waited for: 3 -> 0; matrix products, arithmetic and copies ran while one was open for 2% -> 0% of each run, Pallas kernels for 0% -> 0%
where the time goes in v2:
time: 165 us; the launch traced here: 164 us
  Pallas kernels  160 us (97%)
  local copies, waits for them, and re-layouts  3.02 us (2%)
    pallas_call x1, Pallas kernels, shards(): pl.pallas_call(kernel, out_shape=jax.ShapeDtypeStruct(whole, F32), in_spe...  160 us

profile of v2, /device:TPU:1, one launch (start us, length us, event | category | flops | bytes accessed | tf_op | source)
XLA Modules:
  0.0 163.8 jit_solution(14583733994641604372)
XLA Ops:
  0.0 0.8 eq.49
  0.8 0.1 convert_reduce_fusion
  0.9 0.1 select_reduce_fusion
  1.0 0.1 copy.6
  1.1 0.6 reshape.48.bslot
  1.7 160.5 %shard_map.55 = f32[128,256]{1,0:T(8,128)} custom-call(s32[4,16]{1,0:T(4,128)} %bitcast.6, s32[64]{0:T(128)} %reshape.48.bslot, f32[128,256]{1,0:T(8,128)} %paths_hbm.1, f32[128,256]{1,0:T(8,128)} %dep_hbm.1, s32[128,256]{1,0:T(8,128)} %levels_hbm.1, s32[64,128,128]{2,1,0:T(8,128)} %bitcast.4), custom_call_target="tpu_custom_call" | custom-call | tf_op jit(solution)/shard_map/pallas_call | solution.py:412
  162.2 1.6 copy.8
  (2 shorter events, 0.0 us)

commit v3 on v2

--- a/solution.py
+++ b/solution.py
@@ -14,6 +14,7 @@
 NB = 1
 PR = 80
 QR = TILE - PR
+ORDER = (0, 1, 2, 5, 6, 3, 4, 7)
 FWD = (-5.0, 1365.0)
 BWD = (-44.0, 744.0)
 LN2 = 0.6931471805599453
@@ -35,7 +36,7 @@
 def kernel(
     tsrc, bslot, paths_hbm, dep_hbm, levels_hbm, pattern, out,
     paths_in, dep_in, levels,
-    stage, acat, at, gath, wgt, local, part, paths, total,
+    stage, acat, at, gath, wgtp, wgtq, local, part, paths, total,
     ysend, yrecv, zsend, zrecv, qsend, qrecv, fsend, frecv, csend, crecv, isend, irecv,
     load_sem, in_sem,
     ag_s, ag_r, sib_s, sib_r, y_s, y_r, z_s, z_r, q_s, q_r, f_s, f_r,
@@ -98,8 +99,8 @@
         ref = gath.at[b, lvl, place]
         return move(ref, ref, ag_s.at[b, n], ag_r.at[b, lvl, n], c_dev(n))
 
-    def sib_move(b, lvl, n, place):
-        ref = gath.at[b, lvl, place]
+    def sib_move(b, lvl, n):
+        ref = gath.at[b, lvl, core * 8 + c_to(n, -1)]
         return move(ref, ref, sib_s.at[b, n], sib_r.at[b, lvl, n], sibling)
 
     def y_move(b, lvl, j):
@@ -117,9 +118,12 @@
     def f_move(b, lvl):
         return move(fsend.at[b, 0], frecv.at[b, lvl, 0], f_s.at[b, 0], f_r.at[b, lvl, 0], across)
 
+    def y_sum(b, lvl, j):
+        y_move(b, lvl, j).wait_recv()
+        return part[b, 0, j, :PR] + decode(yrecv[b, lvl, j], FWD)
+
     def z_go(b, lvl, j):
-        y_move(b, lvl, j).wait_recv()
-        v = part[b, 0, j, :PR] + decode(yrecv[b, lvl, j], FWD)
+        v = y_sum(b, lvl, j)
         for m in {3: (1, 0), 4: (2,)}.get(j, ()):
             z_move(b, lvl, m).wait_recv()
             v += decode(zrecv[b, lvl, m], FWD)
@@ -138,25 +142,27 @@
         q_move(b, lvl, j).start()
 
     def fwd_send(b, lvl, value):
-        gath[b, lvl, c] = value.astype(BF16)
+        gath[b, lvl, core * 8 + chip] = value.astype(BF16)
         for n in range(7):
-            ag_move(b, lvl, n, c).start()
-        sib_move(b, lvl, 7, c).start()
+            ag_move(b, lvl, n, core * 8 + chip).start()
+        sib_move(b, lvl, 7).start()
 
     def fwd_pass(b, lvl):
+        local[b, core * 8 + chip] = gath[b, lvl, core * 8 + chip]
         for n in (6, 4, 5, 3, 2, 0, 1):
-            place = c_to(n, -1) * 2 + core
+            place = core * 8 + c_to(n, -1)
             ag_move(b, lvl, n, place).wait_recv()
-            sib_move(b, lvl, n, place).start()
+            sib_move(b, lvl, n).start()
+            local[b, place] = gath[b, lvl, place]
 
     def fwd_tile(b, i):
         rhs = jnp.concatenate([local[b, tsrc[e, i]] for e in range(BAND)], axis=0)
         return jnp.dot(acat[i], rhs, preferred_element_type=F32)
 
     def fwd_work(b, lvl):
-        for n in range(8):
-            sib_move(b, lvl, n, c).wait_recv()
-        local[b] = gath[b, lvl]
+        for n in (7, 6, 4, 5, 3, 2, 0, 1):
+            sib_move(b, lvl, n).wait_recv()
+            local[b, (1 - core) * 8 + c_to(n, -1)] = gath[b, lvl, (1 - core) * 8 + c_to(n, -1)]
 
         def pair(j):
             for k, i in ((1, z_to(j) * 2 + 1 - y), (0, z_to(j) * 2 + y)):
@@ -164,15 +170,18 @@
             ysend[b, j] = encode(part[b, 1, j, :PR], FWD)
             y_move(b, lvl, j).start()
 
-        for j in range(3):
+        for j in ORDER:
             pair(j)
-            q_go(b, lvl, j)
-
-        for j in (5, 6, 3, 4, 7):
-            pair(j)
+            if j < 3:
+                q_go(b, lvl, j)
             if j == 6:
                 q_go(b, lvl, 5)
                 q_go(b, lvl, 6)
+
+        for n in range(7):
+            ag_move(b, lvl, n, chip).wait_send()
+        for k in range(8):
+            sib_move(b, lvl, k).wait_send()
 
     def fwd_mid(b, lvl):
         for j in (0, 1, 2):
@@ -182,7 +191,8 @@
         for j in (5, 6, 3, 4):
             z_go(b, lvl, j)
 
-    def fwd_end(b, lvl):
+    def fwd_end(b, lvl, go):
+        mine = y_sum(b, lvl, 7)
         own = part[b, 0, 7, PR:]
         other = part[b, 1, 7, PR:]
         for j in (6, 5, 4, 3):
@@ -191,26 +201,22 @@
             other += decode(qrecv[b, lvl, j, 1], FWD)
         fsend[b, 0] = encode(other, FWD)
         f_move(b, lvl).start()
-        y_move(b, lvl, 7).wait_recv()
-        mine = part[b, 0, 7, :PR] + decode(yrecv[b, lvl, 7], FWD)
+        total[b, PR:] = own
         for j in (6, 5, 4, 3):
             z_move(b, lvl, j).wait_recv()
             mine += decode(zrecv[b, lvl, j], FWD)
         total[b, :PR] = mine
         f_move(b, lvl).wait()
-        total[b, PR:] = own + decode(frecv[b, lvl, 0], FWD)
-        for j in range(7):
-            q_move(b, lvl, j).wait_send()
-        for n in range(7):
-            ag_move(b, lvl, n, c).wait_send()
-            z_move(b, lvl, n).wait_send()
-        for n in range(8):
-            sib_move(b, lvl, n, c).wait_send()
-            y_move(b, lvl, n).wait_send()
+        total[b, PR:] += decode(frecv[b, lvl, 0], FWD)
         level = lvl + 1
         value = jnp.where(levels_of(b) == level, total[b], 0.0)
         paths[b, level] = value
-        return value
+        go(value)
+        for j in range(7):
+            q_move(b, lvl, j).wait_send()
+            z_move(b, lvl, j).wait_send()
+        for j in range(8):
+            y_move(b, lvl, j).wait_send()
 
     def relay_dev(j):
         return z_dev((2, -2, 1, -1, 2, 1, -1)[j])
@@ -218,20 +224,23 @@
     def origin(j):
         return z_hop((-2, 2, -1, 1, -4, -3, 3)[j])
 
-    def wz_move(b, lvl, j, zz):
-        ref = wgt.at[b, lvl, zz * 2 + y]
-        return move(ref, ref, wz_s.at[b, j], wz_r.at[b, lvl, j], relay_dev(j))
-
-    def wq_move(b, lvl, j, zz):
-        ref = wgt.at[b, lvl, zz * 2 + 1 - y, pl.ds(PR, QR)]
-        return move(ref, ref, wq_s.at[b, j], wq_r.at[b, lvl, j], relay_dev(j))
-
-    def wy_move(b, lvl, j, zz):
-        ref = wgt.at[b, lvl, zz * 2 + y, pl.ds(0, PR)]
-        return move(ref, ref, wy_s.at[b, j], wy_r.at[b, lvl, j], across)
+    def slot_from(j):
+        return {4: 1, 5: 1, 6: 2}.get(j, 0)
+
+    def wz_move(b, lvl, j):
+        src, dst = wgtp.at[b, lvl, 0, slot_from(j)], wgtp.at[b, lvl, 0, 1 + j]
+        return move(src, dst, wz_s.at[b, j], wz_r.at[b, lvl, j], relay_dev(j))
+
+    def wq_move(b, lvl, j):
+        src, dst = wgtq.at[b, lvl, slot_from(j)], wgtq.at[b, lvl, 1 + j]
+        return move(src, dst, wq_s.at[b, j], wq_r.at[b, lvl, j], relay_dev(j))
+
+    def wy_move(b, lvl, g):
+        src, dst = wgtp.at[b, lvl, 0, g], wgtp.at[b, lvl, 1, g]
+        return move(src, dst, wy_s.at[b, g], wy_r.at[b, lvl, g], across)
 
     def wf_move(b, lvl):
-        ref = wgt.at[b, lvl, r, pl.ds(PR, QR)]
+        ref = wgtq.at[b, lvl, 0, y]
         return move(ref, ref, wf_s.at[b, 0], wf_r.at[b, lvl, 0], across)
 
     def c_move(b, lvl, n):
@@ -241,31 +250,47 @@
         return move(isend.at[b, n], irecv.at[b, lvl, n], i_s.at[b, n], i_r.at[b, lvl, n], c_dev(n))
 
     def bwd_send(b, lvl, value):
-        wgt[b, lvl, r] = value.astype(BF16)
+        value = value.astype(BF16)
+        wgtq[b, lvl, 0, y] = value[PR:]
         wf_move(b, lvl).start()
+        wgtp[b, lvl, 0, 0] = value[:PR]
         for j in range(4):
-            wz_move(b, lvl, j, z).start()
-        wy_move(b, lvl, 7, z).start()
+            wz_move(b, lvl, j).start()
+        wy_move(b, lvl, 0).start()
+
+    def keep_p(b, lvl, side, slot):
+        zz = origin(slot - 1) if slot else z
+        local[b, zz * 2 + (1 - y if side else y), :PR] = wgtp[b, lvl, side, slot]
+
+    def keep_q(b, lvl, slot):
+        zz = origin(slot - 1) if slot else z
+        local[b, pl.ds(zz * 2, 2), PR:] = wgtq[b, lvl, slot]
 
     def bwd_pass(b, lvl):
         wf_move(b, lvl).wait_recv()
         for j in range(4):
-            wq_move(b, lvl, j, z).start()
-        def take(go, j):
-            go(b, lvl, j, origin(j)).wait_recv()
+            wq_move(b, lvl, j).start()
+        for j in (2, 3, 0, 1):
+            wz_move(b, lvl, j).wait_recv()
             for m in {0: (4, 5), 1: (6,)}.get(j, ()):
-                go(b, lvl, m, origin(j)).start()
-            if go is wz_move:
-                wy_move(b, lvl, j, origin(j)).start()
-
-        for j in (2, 3, 0, 1):
-            take(wz_move, j)
-        take(wq_move, 0)
-        take(wq_move, 1)
+                wz_move(b, lvl, m).start()
+            wy_move(b, lvl, 1 + j).start()
+        for j in (0, 1):
+            wq_move(b, lvl, j).wait_recv()
+            for m in {0: (4, 5), 1: (6,)}[j]:
+                wq_move(b, lvl, m).start()
+        for slot in range(5):
+            keep_p(b, lvl, 0, slot)
+        for slot in range(3):
+            keep_q(b, lvl, slot)
         for j in (5, 6, 4):
-            take(wz_move, j)
+            wz_move(b, lvl, j).wait_recv()
+            wy_move(b, lvl, 1 + j).start()
+        for slot in range(5, 8):
+            keep_p(b, lvl, 0, slot)
         for j in (2, 3, 5, 6, 4):
-            take(wq_move, j)
+            wq_move(b, lvl, j).wait_recv()
+            keep_q(b, lvl, 1 + j)
 
     def bwd_tile(b, t):
         slots = [bslot[t * BAND + e] for e in range(BAND)]
@@ -274,71 +299,72 @@
         return jnp.dot(lhs, rhs, preferred_element_type=F32)
 
     def bwd_work(b, lvl):
-        for j in range(8):
-            wy_move(b, lvl, j, z).wait_recv()
-        local[b] = wgt[b, lvl]
-
-        @pl.loop(0, 8)
-        def _(n):
-            csend[b, n] = encode(bwd_tile(b, c_to(n) * 2 + 1 - core), BWD)
-            c_move(b, lvl, n).start()
-
-        @pl.loop(0, 8)
-        def _(n):
+        for slot in (0, 3, 4, 1, 2, 6, 7, 5):
+            wy_move(b, lvl, slot).wait_recv()
+            keep_p(b, lvl, 1, slot)
+
+        def sums(n):
             part[b, 0, n] = bwd_tile(b, c_to(n) * 2 + core)
-
-    def bwd_mid(b, lvl):
-        for n in range(7):
             c_move(b, lvl, n).wait_recv()
             v = part[b, 0, n] + decode(crecv[b, lvl, n], BWD)
+            if n == 7:
+                total[b] = v
+                return
             isend[b, n] = encode(v, BWD)
             i_move(b, lvl, n).start()
 
-        c_move(b, lvl, 7).wait_recv()
-        total[b] = part[b, 0, 7] + decode(crecv[b, lvl, 7], BWD)
-
-    def bwd_end(b, lvl):
+        ahead = 3
+        for n in range(8 + ahead):
+            if n < 8:
+                csend[b, n] = encode(bwd_tile(b, c_to(n) * 2 + 1 - core), BWD)
+                c_move(b, lvl, n).start()
+            if n >= ahead:
+                sums(n - ahead)
+        for j in range(7):
+            wz_move(b, lvl, j).wait_send()
+            wq_move(b, lvl, j).wait_send()
+        for g in range(8):
+            wy_move(b, lvl, g).wait_send()
+        wf_move(b, lvl).wait_send()
+
+    def bwd_end(b, lvl, go):
+        level = 2 - lvl
         for n in (6, 4, 5, 3, 2, 0, 1):
             i_move(b, lvl, n).wait_recv()
             total[b] += decode(irecv[b, lvl, n], BWD)
+        mask = levels_of(b) == level
+        counts = paths[b, level]
+        delta = jnp.where(mask, counts * total[b], 0.0)
+        go(jnp.where(mask, 1.0 + delta, 0.0) / jnp.maximum(counts, 1.0))
+        out[:, b * lanes : (b + 1) * lanes] += delta
         for n in range(7):
-            wz_move(b, lvl, n, z).wait_send()
-            wq_move(b, lvl, n, z).wait_send()
             i_move(b, lvl, n).wait_send()
         for n in range(8):
-            wy_move(b, lvl, n, z).wait_send()
             c_move(b, lvl, n).wait_send()
-        wf_move(b, lvl).wait_send()
-        level = 2 - lvl
-        mask = levels_of(b) == level
-        delta = jnp.where(mask, paths[b, level] * total[b], 0.0)
-        out[:, b * lanes : (b + 1) * lanes] += delta
-        return jnp.where(mask, 1.0 + delta, 0.0) / jnp.maximum(paths[b, level], 1.0)
 
     def levels_of(b):
         return levels[:, b * lanes : (b + 1) * lanes]
 
     def fwd_next(b, lvl):
-        value = fwd_end(b, lvl)
-
-        @pl.when(lvl < LVLS - 1)
-        def _():
-            fwd_send(b, lvl + 1, value)
-
-        @pl.when(lvl == LVLS - 1)
-        def _():
-            turn(b, value)
-
-    def turn(b, value):
-        top = jnp.where(levels_of(b) == 3, 1.0 + dep_in[:, b * lanes : (b + 1) * lanes], 0.0)
-        bwd_send(b, 0, top / jnp.maximum(value, 1.0))
+        def go(value):
+            @pl.when(lvl < LVLS - 1)
+            def _():
+                fwd_send(b, lvl + 1, value)
+
+            @pl.when(lvl == LVLS - 1)
+            def _():
+                top = 1.0 + dep_in[:, b * lanes : (b + 1) * lanes]
+                bwd_send(b, 0, jnp.where(levels_of(b) == 3, top, 0.0) / jnp.maximum(value, 1.0))
+
+        fwd_end(b, lvl, go)
 
     def bwd_next(b, lvl):
-        value = bwd_end(b, lvl)
-
-        @pl.when(lvl < LVLS - 1)
-        def _():
-            bwd_send(b, lvl + 1, value)
+        def go(value):
+            @pl.when(lvl < LVLS - 1)
+            def _():
+                bwd_send(b, lvl + 1, value)
+
+        bwd_end(b, lvl, go)
 
     inputs[0].wait()
     inputs[1].wait()
@@ -375,7 +401,7 @@
         return body
 
     pl.loop(0, LVLS)(each(fwd_pass, fwd_work, fwd_mid, fwd_next))
-    pl.loop(0, LVLS)(each(bwd_pass, bwd_work, bwd_mid, bwd_next))
+    pl.loop(0, LVLS)(each(bwd_pass, bwd_work, bwd_next))
 
 
 def slots_by_source(flat):
@@ -392,6 +418,7 @@
     rows, sources = paths_in.shape
     by_slot = tile_src[0, 0].T
     back = slots_by_source(by_slot.reshape(-1))
+    by_slot = by_slot % 2 * 8 + by_slot // 2
     pattern = pattern.reshape(TILES * BAND, TILE, TILE)
     vmem, smem, hbm = (
         pl.BlockSpec(memory_space=m) for m in (pltpu.VMEM, pltpu.SMEM, pltpu.HBM)
@@ -422,7 +449,8 @@
             pltpu.VMEM((TILES, TILE, BAND * TILE), BF16),
             pltpu.VMEM((TILES * BAND, TILE, TILE), BF16),
             pltpu.VMEM((NB, LVLS, TILES, *block), BF16),
-            pltpu.VMEM((NB, LVLS, TILES, *block), BF16),
+            pltpu.VMEM((NB, LVLS, 2, 8, PR, block[1]), BF16),
+            pltpu.VMEM((NB, LVLS, 8, 2, QR, block[1]), BF16),
             pltpu.VMEM((NB, TILES, *block), BF16),
             pltpu.VMEM((NB, 2, 8, *block), F32),
             pltpu.VMEM((NB, 4, *block), F32),

time: 165 us -> 164 us (level)
  no operation moved by 1% of the time
where the time goes in v3:
time: 164 us
  Pallas kernels  159 us (97%)
  local copies, waits for them, and re-layouts  3.01 us (2%)
    pallas_call x1, Pallas kernels, shards(): pl.pallas_call(kernel, out_shape=jax.ShapeDtypeStruct(whole, F32), in_spe...  159 us

profile of v3, /device:TPU:1, one launch (start us, length us, event | category | flops | bytes accessed | tf_op | source)
XLA Modules:
  0.0 163.6 jit_solution(10222052488464472135)
XLA Ops:
  0.0 0.8 eq.51
  0.8 0.1 convert_reduce_fusion
  0.9 0.1 select_reduce_fusion
  1.0 1.3 fusion.2.tsrc
  2.3 0.1 copy.6
  2.4 0.6 reshape.48.bslot
  3.0 159.0 %shard_map.55 = f32[128,256]{1,0:T(8,128)} custom-call(s32[4,16]{1,0:T(4,128)} %fusion.2.tsrc, s32[64]{0:T(128)} %reshape.48.bslot, f32[128,256]{1,0:T(8,128)} %paths_hbm.1, f32[128,256]{1,0:T(8,128)} %dep_hbm.1, s32[128,256]{1,0:T(8,128)} %levels_hbm.1, s32[64,128,128]{2,1,0:T(8,128)} %bitcast.5), custom_call_target="tpu_custom_call" | custom-call | tf_op jit(solution)/shard_map/pallas_call | solution.py:439
  162.0 1.6 copy.8
  (2 shorter events, 0.0 us)

commit v4 on v3

--- a/solution.py
+++ b/solution.py
@@ -11,7 +11,7 @@
 ZS, XS, HI = 8, 4, 2
 TILE, BAND, TILES = 128, 4, 16
 LVLS = 3
-NB = 1
+NB = 2
 PR = 80
 QR = TILE - PR
 ORDER = (0, 1, 2, 5, 6, 3, 4, 7)
@@ -167,13 +167,13 @@
         def pair(j):
             for k, i in ((1, z_to(j) * 2 + 1 - y), (0, z_to(j) * 2 + y)):
                 part[b, k, j] = fwd_tile(b, i)
+            if j < 3:
+                q_go(b, lvl, j)
             ysend[b, j] = encode(part[b, 1, j, :PR], FWD)
             y_move(b, lvl, j).start()
 
         for j in ORDER:
             pair(j)
-            if j < 3:
-                q_go(b, lvl, j)
             if j == 6:
                 q_go(b, lvl, 5)
                 q_go(b, lvl, 6)
@@ -183,16 +183,23 @@
         for k in range(8):
             sib_move(b, lvl, k).wait_send()
 
-    def fwd_mid(b, lvl):
+    def fwd_far(b, lvl):
         for j in (0, 1, 2):
             z_go(b, lvl, j)
+
+    def fwd_joined_late(b, lvl):
         for j in (3, 4):
             q_go(b, lvl, j)
-        for j in (5, 6, 3, 4):
+
+    def fwd_near(b, lvl):
+        for j in (5, 6):
             z_go(b, lvl, j)
 
-    def fwd_end(b, lvl, go):
-        mine = y_sum(b, lvl, 7)
+    def fwd_joined(b, lvl):
+        for j in (3, 4):
+            z_go(b, lvl, j)
+
+    def fwd_late(b, lvl):
         own = part[b, 0, 7, PR:]
         other = part[b, 1, 7, PR:]
         for j in (6, 5, 4, 3):
@@ -202,6 +209,9 @@
         fsend[b, 0] = encode(other, FWD)
         f_move(b, lvl).start()
         total[b, PR:] = own
+
+    def fwd_end(b, lvl, go):
+        mine = y_sum(b, lvl, 7)
         for j in (6, 5, 4, 3):
             z_move(b, lvl, j).wait_recv()
             mine += decode(zrecv[b, lvl, j], FWD)
@@ -270,11 +280,15 @@
         wf_move(b, lvl).wait_recv()
         for j in range(4):
             wq_move(b, lvl, j).start()
+
+    def bwd_near(b, lvl):
         for j in (2, 3, 0, 1):
             wz_move(b, lvl, j).wait_recv()
             for m in {0: (4, 5), 1: (6,)}.get(j, ()):
                 wz_move(b, lvl, m).start()
             wy_move(b, lvl, 1 + j).start()
+
+    def bwd_late(b, lvl):
         for j in (0, 1):
             wq_move(b, lvl, j).wait_recv()
             for m in {0: (4, 5), 1: (6,)}[j]:
@@ -283,11 +297,15 @@
             keep_p(b, lvl, 0, slot)
         for slot in range(3):
             keep_q(b, lvl, slot)
+
+    def bwd_far(b, lvl):
         for j in (5, 6, 4):
             wz_move(b, lvl, j).wait_recv()
             wy_move(b, lvl, 1 + j).start()
         for slot in range(5, 8):
             keep_p(b, lvl, 0, slot)
+
+    def bwd_rest(b, lvl):
         for j in (2, 3, 5, 6, 4):
             wq_move(b, lvl, j).wait_recv()
             keep_q(b, lvl, 1 + j)
@@ -400,8 +418,8 @@
 
         return body
 
-    pl.loop(0, LVLS)(each(fwd_pass, fwd_work, fwd_mid, fwd_next))
-    pl.loop(0, LVLS)(each(bwd_pass, bwd_work, bwd_next))
+    pl.loop(0, LVLS)(each(fwd_pass, fwd_work, fwd_far, fwd_joined_late, fwd_near, fwd_joined, fwd_late, fwd_next))
+    pl.loop(0, LVLS)(each(bwd_pass, bwd_near, bwd_late, bwd_far, bwd_rest, bwd_work, bwd_next))
 
 
 def slots_by_source(flat):

time: 164 us -> 162 us (0.988)
  Pallas kernels: 159 us -> 157 us
    pallas_call x1, Pallas kernels: 159 us -> 157 us  [shards(): pl.pallas_call(kernel, out_shape=jax.ShapeDtypeStruct(whole, F32), in_spe...]
where the time goes in v4:
time: 162 us; the launch traced here: 161 us
  Pallas kernels  157 us (97%)
  local copies, waits for them, and re-layouts  3.01 us (2%)
    pallas_call x1, Pallas kernels, shards(): pl.pallas_call(kernel, out_shape=jax.ShapeDtypeStruct(whole, F32), in_spe...  157 us

profile of v4, /device:TPU:1, one launch (start us, length us, event | category | flops | bytes accessed | tf_op | source)
XLA Modules:
  0.0 161.3 jit_solution(5581616172553364790)
XLA Ops:
  0.0 0.8 eq.51
  0.8 0.1 convert_reduce_fusion
  0.9 0.1 select_reduce_fusion
  1.0 1.3 fusion.2.tsrc
  2.3 0.1 copy.6
  2.4 0.6 reshape.48.bslot
  3.0 156.8 %shard_map.55 = f32[128,256]{1,0:T(8,128)} custom-call(s32[4,16]{1,0:T(4,128)} %fusion.2.tsrc, s32[64]{0:T(128)} %reshape.48.bslot, f32[128,256]{1,0:T(8,128)} %paths_hbm.1, f32[128,256]{1,0:T(8,128)} %dep_hbm.1, s32[128,256]{1,0:T(8,128)} %levels_hbm.1, s32[64,128,128]{2,1,0:T(8,128)} %bitcast.5), custom_call_target="tpu_custom_call" | custom-call | tf_op jit(solution)/shard_map/pallas_call | solution.py:457
  159.8 1.6 copy.8
  (2 shorter events, 0.0 us)

commit v5 on v4

--- a/solution.py
+++ b/solution.py
@@ -404,9 +404,16 @@
         for e in range(BAND):
             tile = stage[i, e].astype(F32).astype(BF16)
             acat[i, :, e * TILE : (e + 1) * TILE] = tile
-            at[e * TILES + i] = lax.dot_general(
-                eye, tile, (((1,), (1,)), ((), ())), preferred_element_type=F32
-            ).astype(BF16)
+
+    def transpose_half(lvl):
+        @pl.loop(0, TILES // 2)
+        def _(k):
+            i = (lvl - 1) * (TILES // 2) + k
+            for e in range(BAND):
+                tile = acat[i, :, e * TILE : (e + 1) * TILE]
+                at[e * TILES + i] = lax.dot_general(
+                    eye, tile, (((1,), (1,)), ((), ())), preferred_element_type=F32
+                ).astype(BF16)
 
     batches = range(NB)
 
@@ -418,7 +425,11 @@
 
         return body
 
-    pl.loop(0, LVLS)(each(fwd_pass, fwd_work, fwd_far, fwd_joined_late, fwd_near, fwd_joined, fwd_late, fwd_next))
+    def fwd_turn(b, lvl):
+        if b == 0:
+            pl.when(lvl > 0)(lambda: transpose_half(lvl))
+
+    pl.loop(0, LVLS)(each(fwd_turn, fwd_pass, fwd_work, fwd_far, fwd_joined_late, fwd_near, fwd_joined, fwd_late, fwd_next))
     pl.loop(0, LVLS)(each(bwd_pass, bwd_near, bwd_late, bwd_far, bwd_rest, bwd_work, bwd_next))
 
 

time: 162 us -> 161 us (level)
  no operation moved by 1% of the time
where the time goes in v5:
time: 161 us
  Pallas kernels  156 us (97%)
  local copies, waits for them, and re-layouts  3.01 us (2%)
    pallas_call x1, Pallas kernels, shards(): pl.pallas_call(kernel, out_shape=jax.ShapeDtypeStruct(whole, F32), in_spe...  156 us

profile of v5, /device:TPU:1, one launch (start us, length us, event | category | flops | bytes accessed | tf_op | source)
XLA Modules:
  0.0 161.1 jit_solution(18116070398759314495)
XLA Ops:
  0.0 0.8 eq.51
  0.8 0.1 convert_reduce_fusion
  0.9 0.1 select_reduce_fusion
  1.0 1.3 fusion.2.tsrc
  2.3 0.1 copy.6
  2.4 0.6 reshape.48.bslot
  3.0 156.5 %shard_map.55 = f32[128,256]{1,0:T(8,128)} custom-call(s32[4,16]{1,0:T(4,128)} %fusion.2.tsrc, s32[64]{0:T(128)} %reshape.48.bslot, f32[128,256]{1,0:T(8,128)} %paths_hbm.1, f32[128,256]{1,0:T(8,128)} %dep_hbm.1, s32[128,256]{1,0:T(8,128)} %levels_hbm.1, s32[64,128,128]{2,1,0:T(8,128)} %bitcast.5), custom_call_target="tpu_custom_call" | custom-call | tf_op jit(solution)/shard_map/pallas_call | solution.py:468
  159.5 1.6 copy.8
  (2 shorter events, 0.0 us)
